TPU v7x, 32 devices: a whole 2x2x4 slice. The times are simulated.
32 devices in a mesh: swath: 2 (over y), shot: 4 (over z), rec: 2 (over x), tr: 2 (over core).
Axes of the slice: x: 2, y: 2, z: 4, core: 2. Of those that a mesh axis runs over, the one named last changes fastest.
Arguments:
- model_init: float32 [8, 512, 2048], P(('swath', 'shot'), None, ('rec', 'tr')), parts along dimension 0, may hold values from -6 to 6
- record: float32 [512, 8192], P(('rec', 'tr'), ('swath', 'shot')), parts along dimension 1, may hold values from -12 to 12
- activation_dither: int32 [8], P(('swath', 'shot')), parts along dimension 0, may hold values from 0 to 511
Outputs:
- model: float32 [8, 512, 2048], P(('swath', 'shot'), None, ('rec', 'tr')), parts along dimension 0
- residual: float32 [512, 8192], P(('rec', 'tr'), ('swath', 'shot')), parts along dimension 1
There are 2 independent parts, one for each index of `swath`. A program takes and returns all parts, laid end to end along the dimension named above; each array names one. Nothing has to cross between parts.
All inputs are finite; a program needn't handle non-finite values.
Results may differ from a plain program's by a relative error of at most 0.012.
The roundings to bfloat16 on the way count: a program that leaves them out, or rounds other values in their place, can miss the bound.
Values may be sent and summed in bfloat16 or wider, within the bound.
A program may use at most 64 MiB of HBM per device.

v0:
```python
import math

import jax
import jax.numpy as jnp
from jax import lax
from jax.sharding import PartitionSpec as P

ITERS = 2


def passed_along(value, axis, steps):
    count = lax.axis_size(axis)
    first, last = (max(0, -steps), min(count, count - steps))
    return lax.ppermute(value, axis, [(source, source + steps) for source in range(first, last)])


def cosine_table(order):
    emitter_location = jnp.arange(order, dtype=jnp.int32)
    phase = (2 * emitter_location[None, :] + 1) * emitter_location[:, None] % (4 * order)
    table = jnp.cos(math.pi * phase.astype(jnp.float32) / (2.0 * order)) * math.sqrt(2.0 / order)
    table = table * jnp.where(emitter_location[:, None] == 0, math.sqrt(0.5), 1.0).astype(
        jnp.float32
    )
    return table.astype(jnp.bfloat16)


def shards(model_init, record, activation_dither):
    shots_dev, traces, freq_dev = model_init.shape
    traces_dev, window = record.shape
    time_len = freq_dev * lax.axis_size(("rec", "tr"))
    spacing = time_len // 2
    jitter = time_len // 4
    hops = (time_len + jitter - spacing + window - 1) // window
    margin = (hops + 1) * window
    time_table = cosine_table(time_len)
    trace_table = cosine_table(traces)
    starts = jnp.arange(shots_dev, dtype=jnp.int32) * spacing + activation_dither - jitter + window
    width = window + margin
    model = model_init
    residual = record
    for sweep in range(ITERS):
        spread = jnp.einsum(
            "skf,kr->srf",
            model.astype(jnp.bfloat16),
            trace_table,
            preferred_element_type=jnp.float32,
        ).astype(jnp.bfloat16)
        shot_data = jnp.einsum(
            "srf,ft->srt",
            lax.all_to_all(spread, ("rec", "tr"), split_axis=1, concat_axis=2, tiled=True),
            time_table,
            preferred_element_type=jnp.float32,
        )
        buffer = jnp.zeros((traces_dev, width), jnp.float32)
        buffer = lax.dynamic_update_slice_in_dim(buffer, shot_data[0], starts[0], 1)
        predicted = buffer[:, window : 2 * window]
        predicted = predicted + passed_along(buffer[:, :window], "shot", -1)
        for hop in range(1, hops + 1):
            predicted = predicted + passed_along(
                buffer[:, (hop + 1) * window : (hop + 2) * window], "shot", hop
            )
        residual = record - predicted
        narrow = residual.astype(jnp.bfloat16)
        earlier = passed_along(narrow, "shot", 1)
        later = [passed_along(narrow, "shot", -hop) for hop in range(1, hops + 1)]
        padded = jnp.concatenate([earlier, narrow] + later, axis=1)
        emitter_pieces = jnp.stack(
            [lax.dynamic_slice_in_dim(padded, starts[0], time_len, 1)], axis=0
        )
        spectra = jnp.einsum(
            "srt,ft->srf", emitter_pieces, time_table, preferred_element_type=jnp.float32
        ).astype(jnp.bfloat16)
        grad = jnp.einsum(
            "srf,kr->skf",
            lax.all_to_all(spectra, ("rec", "tr"), split_axis=2, concat_axis=1, tiled=True),
            trace_table,
            preferred_element_type=jnp.float32,
        )
        value = model + 0.5 * grad
        model = jnp.sign(value) * jnp.maximum(jnp.abs(value) - 0.3, 0.0)
    return (model, residual)


def solution(mesh):
    return jax.shard_map(
        shards,
        mesh=mesh,
        in_specs=(
            P(("swath", "shot"), None, ("rec", "tr")),
            P(("rec", "tr"), ("swath", "shot")),
            P(("swath", "shot")),
        ),
        out_specs=(P(("swath", "shot"), None, ("rec", "tr")), P(("rec", "tr"), ("swath", "shot"))),
        check_vma=False,
    )
```

profile of v0, /device:TPU:8, one launch (start us, length us, event | category | flops | bytes accessed | tf_op | source)
XLA Modules:
  0.0 508.9 jit_solution(16420411725242029010)
XLA Ops:
  0.7 5.4 %fusion.33 = bf16[1,512,512]{2,1,0:T(8,128)(2,1)S(1)} fusion(f32[1,512,512]{2,1,0:T(8,128)} %param.3, f32[512]{0:T(512)S(1)} %select_multiply_fusion.1, s32[512]{0:T(512)S(1)} %multiply_add_fusion.1), kind=kOutput, calls=%fused_computation.31 | convolution fusion | flops 273154048 | bytes 1576960 | tf_op jit(solution)/shard_map/skf,kr->srf/dot_general | solution.py:42
  16.7 8.1 %all-to-all-done = bf16[4,2,32768]{2,1,0:T(2,128)(2,1)S(1)} async-done(((bf16[4,2,32768]{2,1,0:T(2,128)(2,1)}), bf16[4,2,32768]{2,1,0:T(2,128)(2,1)S(1)}, u32[]{:S(2)}, u32[]{:S(2)}) %all-to-all-start) | async-done | bytes 524320 | tf_op jit(solution)/shard_map/all_to_all | solution.py:50
  25.8 74.5 %fusion.15 = f32[128,2048]{1,0:T(8,128)} fusion(bf16[128,2048]{0,1:T(8,128)(2,1)S(1)} %bitcast.77, f32[2048]{0:T(1024)S(1)} %select_multiply_fusion, s32[2048]{0:T(1024)S(1)} %multiply_add_fusion), kind=kOutput, calls=%fused_computation.15 | convolution fusion | flops 1140850688 | bytes 1589248 | tf_op jit(solution)/shard_map/srf,ft->srt/dot_general | solution.py:48
  100.5 6.1 %dynamic_update_slice.6 = f32[128,4096]{1,0:T(8,128)S(1)} dynamic-update-slice(f32[128,4096]{1,0:T(8,128)S(1)} %broadcast.87.clone, f32[128,2048]{1,0:T(8,128)} %fusion.15, s32[]{:T(128)} %constant.26.clone.1, s32[]{:T(128)S(6)} %select_n.65) | dynamic-update-slice | bytes 2097156 | tf_op jit(solution)/shard_map/dynamic_update_slice | solution.py:55
  108.7 4.8 collective-permute-start.2
  115.5 6.7 %collective-permute-done = f32[128,1024]{1,0:T(8,128)S(1)} collective-permute-done((f32[128,1024]{1,0:T(8,128)S(1)}, f32[128,1024]{1,0:T(8,128)S(1)}, u32[]{:S(2)}, u32[]{:S(2)}) %collective-permute-start) | collective-permute-done | bytes 524320 | tf_op jit(solution)/shard_map/ppermute | solution.py:14
  122.2 13.5 %collective-permute-done.2 = f32[128,1024]{1,0:T(8,128)S(1)} collective-permute-done((f32[128,1024]{1,0:T(8,128)S(1)}, f32[128,1024]{1,0:T(8,128)S(1)}, u32[]{:S(2)}, u32[]{:S(2)}) %collective-permute-start.2) | collective-permute-done | bytes 524320 | tf_op jit(solution)/shard_map/ppermute | solution.py:14
  135.6 11.1 %collective-permute-done.1 = f32[128,1024]{1,0:T(8,128)S(1)} collective-permute-done((f32[128,1024]{1,0:T(8,128)S(1)}, f32[128,1024]{1,0:T(8,128)S(1)}, u32[]{:S(2)}, u32[]{:S(2)}) %collective-permute-start.1) | collective-permute-done | bytes 524320 | tf_op jit(solution)/shard_map/ppermute | solution.py:14
  150.2 4.4 collective-permute-start.3
  159.0 9.5 %collective-permute-done.4 = bf16[128,1024]{1,0:T(8,128)(2,1)S(1)} collective-permute-done((bf16[128,1024]{1,0:T(8,128)(2,1)S(1)}, bf16[128,1024]{1,0:T(8,128)(2,1)S(1)}, u32[]{:S(2)}, u32[]{:S(2)}) %collective-permute-start.4) | collective-permute-done | bytes 262176 | tf_op jit(solution)/shard_map/ppermute | solution.py:14
  169.2 63.7 %fusion.26 = bf16[1,128,2048]{2,1,0:T(8,128)(2,1)S(1)} fusion(f32[2048]{0:T(1024)S(1)} %select_multiply_fusion, s32[2048]{0:T(1024)S(1)} %multiply_add_fusion, bf16[128,2048]{1,0:T(8,128)(2,1)S(1)} %fusion.120), kind=kOutput, calls=%fused_computation.19 | convolution fusion | flops 1141112832 | bytes 1064960 | tf_op jit(solution)/shard_map/srt,ft->srf/dot_general | solution.py:70
  233.7 11.5 %reduce.1 = bf16[2048,128]{1,0:T(8,128)(2,1)S(1)} reduce(bf16[2048,1,128]{2,1,0:T(2,128)(2,1)S(1)} %bitcast.70, bf16[]{:T(256)} %broadcast.121), dimensions={1}, to_apply=%bitcast.45.reduce_sub_computation | reduce | bytes 1048578
  245.3 11.2 %all_to_all.60 = bf16[4,2,32768]{2,1,0:T(2,128)(2,1)S(1)} all-to-all(bf16[4,2,32768]{2,1,0:T(2,128)(2,1)S(1)} %reshape.86), channel_id=1, replica_groups=mesh['swath'=2,'shot'=4,'rec'=2,'tr'=2] {'rec','tr'}, dimensions={0} | all-to-all | bytes 1048576 | tf_op jit(solution)/shard_map/all_to_all | solution.py:75
  272.5 11.2 %all_to_all.61 = bf16[4,2,32768]{2,1,0:T(2,128)(2,1)S(1)} all-to-all(bf16[4,2,32768]{2,1,0:T(2,128)(2,1)S(1)} %reshape.88), channel_id=1, replica_groups=mesh['swath'=2,'shot'=4,'rec'=2,'tr'=2] {'rec','tr'}, dimensions={0} | all-to-all | bytes 1048576 | tf_op jit(solution)/shard_map/all_to_all | solution.py:50
  284.7 63.7 %fusion.11 = f32[128,2048]{1,0:T(8,128)} fusion(bf16[128,2048]{0,1:T(8,128)(2,1)S(1)} %bitcast.79, f32[2048]{0:T(1024)S(1)} %select_multiply_fusion, s32[2048]{0:T(1024)S(1)} %multiply_add_fusion), kind=kOutput, calls=%fused_computation.13 | convolution fusion | flops 1140850688 | bytes 1589248 | tf_op jit(solution)/shard_map/srf,ft->srt/dot_general | solution.py:48
  348.6 6.1 %dynamic_update_slice.7 = f32[128,4096]{1,0:T(8,128)S(1)} dynamic-update-slice(f32[128,4096]{1,0:T(8,128)S(1)} %broadcast.87, f32[128,2048]{1,0:T(8,128)} %fusion.11, s32[]{:T(128)} %constant.26.clone.1, s32[]{:T(128)S(6)} %select_n.65) | dynamic-update-slice | bytes 2097156 | tf_op jit(solution)/shard_map/dynamic_update_slice | solution.py:55
  362.0 8.0 %collective-permute-done.6 = f32[128,1024]{1,0:T(8,128)S(1)} collective-permute-done((f32[128,1024]{1,0:T(8,128)S(1)}, f32[128,1024]{1,0:T(8,128)S(1)}, u32[]{:S(2)}, u32[]{:S(2)}) %collective-permute-start.6) | collective-permute-done | bytes 524320 | tf_op jit(solution)/shard_map/ppermute | solution.py:14
  370.1 13.1 %collective-permute-done.8 = f32[128,1024]{1,0:T(8,128)S(1)} collective-permute-done((f32[128,1024]{1,0:T(8,128)S(1)}, f32[128,1024]{1,0:T(8,128)S(1)}, u32[]{:S(2)}, u32[]{:S(2)}) %collective-permute-start.8) | collective-permute-done | bytes 524320 | tf_op jit(solution)/shard_map/ppermute | solution.py:14
  383.2 9.4 %collective-permute-done.7 = f32[128,1024]{1,0:T(8,128)S(1)} collective-permute-done((f32[128,1024]{1,0:T(8,128)S(1)}, f32[128,1024]{1,0:T(8,128)S(1)}, u32[]{:S(2)}, u32[]{:S(2)}) %collective-permute-start.7) | collective-permute-done | bytes 524320 | tf_op jit(solution)/shard_map/ppermute | solution.py:14
  405.6 7.7 %collective-permute-done.10 = bf16[128,1024]{1,0:T(8,128)(2,1)S(1)} collective-permute-done((bf16[128,1024]{1,0:T(8,128)(2,1)S(1)}, bf16[128,1024]{1,0:T(8,128)(2,1)S(1)}, u32[]{:S(2)}, u32[]{:S(2)}) %collective-permute-start.10) | collective-permute-done | bytes 262176 | tf_op jit(solution)/shard_map/ppermute | solution.py:14
  414.1 63.7 %fusion.23 = bf16[1,128,2048]{2,1,0:T(8,128)(2,1)S(1)} fusion(f32[2048]{0:T(1024)S(1)} %select_multiply_fusion, s32[2048]{0:T(1024)S(1)} %multiply_add_fusion, bf16[128,2048]{1,0:T(8,128)(2,1)S(1)} %fusion.118), kind=kOutput, calls=%fused_computation.18 | convolution fusion | flops 1141112832 | bytes 1064960 | tf_op jit(solution)/shard_map/srt,ft->srf/dot_general | solution.py:70
  478.5 11.7 %reduce.3 = bf16[2048,128]{1,0:T(8,128)(2,1)S(1)} reduce(bf16[2048,1,128]{2,1,0:T(2,128)(2,1)S(1)} %bitcast.69, bf16[]{:T(256)} %broadcast.121), dimensions={1}, to_apply=%bitcast.49.reduce_sub_computation | reduce | bytes 1048578
  490.4 11.2 %all_to_all.62 = bf16[4,2,32768]{2,1,0:T(2,128)(2,1)S(1)} all-to-all(bf16[4,2,32768]{2,1,0:T(2,128)(2,1)S(1)} %reshape.90), channel_id=1, replica_groups=mesh['swath'=2,'shot'=4,'rec'=2,'tr'=2] {'rec','tr'}, dimensions={0} | all-to-all | bytes 1048576 | tf_op jit(solution)/shard_map/all_to_all | solution.py:75
  502.9 5.6 %maximum_multiply_fusion = f32[1,512,512]{2,1,0:T(8,128)} fusion(f32[1,512,512]{2,1,0:T(8,128)S(1)} %copy-done.3, bf16[512,512]{1,0:T(8,128)(2,1)S(1)} %bitcast.76, f32[512]{0:T(512)S(1)} %select_multiply_fusion.1, s32[512]{0:T(512)S(1)} %multiply_add_fusion.1), kind=kOutput, calls=%fused_computation.47 | convolution fusion | flops 274464768 | bytes 2625536 | tf_op jit(solution)/shard_map/srf,kr->skf/dot_general | solution.py:73
  (60 shorter events, 64.8 us)
Async XLA Ops:
  12.5 12.3 %all-to-all-start = ((bf16[4,2,32768]{2,1,0:T(2,128)(2,1)}), bf16[4,2,32768]{2,1,0:T(2,128)(2,1)S(1)}, u32[]{:S(2)}, u32[]{:S(2)}) async-start(bf16[4,2,32768]{2,1,0:T(2,128)(2,1)} %reshape.84), calls=%async_computation | async-start | bytes 1048576 | tf_op jit(solution)/shard_map/all_to_all | solution.py:50
  106.6 40.1 %copy-start = (f32[128,1024]{1,0:T(8,128)S(1)}, f32[128,1024]{1,0:T(8,128)}, u32[]{:S(2)}) copy-start(f32[128,1024]{1,0:T(8,128)} %param.4) | copy-start | bytes 1572868
  106.8 15.4 %collective-permute-start = (f32[128,1024]{1,0:T(8,128)S(1)}, f32[128,1024]{1,0:T(8,128)S(1)}, u32[]{:S(2)}, u32[]{:S(2)}) collective-permute-start(f32[128,1024]{1,0:T(8,128)S(1)} %get-tuple-element.7), channel_id=1, source_target_pairs={{4,0},{8,4},{12,8},{5,1},{9,5},{13,9},{6,2},{10,6},{14,10},{7,3},{... | collective-permute-start | bytes 1572872 | tf_op jit(solution)/shard_map/ppermute | solution.py:14
  108.7 26.9 %collective-permute-start.2 = (f32[128,1024]{1,0:T(8,128)S(1)}, f32[128,1024]{1,0:T(8,128)S(1)}, u32[]{:S(2)}, u32[]{:S(2)}) collective-permute-start(f32[128,1024]{1,0:T(8,128)S(1)} %get-tuple-element.8), channel_id=1, source_target_pairs={{0,8},{4,12},{1,9},{5,13},{2,10},{6,14},{3,11},{7,15},{16,24},{20,... | collective-permute-start | bytes 1572872 | tf_op jit(solution)/shard_map/ppermute | solution.py:14
  113.6 33.2 %collective-permute-start.1 = (f32[128,1024]{1,0:T(8,128)S(1)}, f32[128,1024]{1,0:T(8,128)S(1)}, u32[]{:S(2)}, u32[]{:S(2)}) collective-permute-start(f32[128,1024]{1,0:T(8,128)S(1)} %get-tuple-element.9), channel_id=1, source_target_pairs={{0,4},{4,8},{8,12},{1,5},{5,9},{9,13},{2,6},{6,10},{10,14},{3,7},{... | collective-permute-start | bytes 1572872 | tf_op jit(solution)/shard_map/ppermute | solution.py:14
  147.0 12.0 %collective-permute-start.5 = (bf16[128,1024]{1,0:T(8,128)(2,1)S(1)}, bf16[128,1024]{1,0:T(8,128)(2,1)S(1)}, u32[]{:S(2)}, u32[]{:S(2)}) collective-permute-start(bf16[128,1024]{1,0:T(8,128)(2,1)S(1)} %fusion.58), channel_id=1, source_target_pairs={{8,0},{12,4},{9,1},{13,5},{10,2},{14,6},{11,3},{15,7},{24,16},{28,... | collective-permute-start | bytes 786440 | tf_op jit(solution)/shard_map/ppermute | solution.py:14
  148.3 20.2 %collective-permute-start.4 = (bf16[128,1024]{1,0:T(8,128)(2,1)S(1)}, bf16[128,1024]{1,0:T(8,128)(2,1)S(1)}, u32[]{:S(2)}, u32[]{:S(2)}) collective-permute-start(bf16[128,1024]{1,0:T(8,128)(2,1)S(1)} %fusion.58), channel_id=1, source_target_pairs={{4,0},{8,4},{12,8},{5,1},{9,5},{13,9},{6,2},{10,6},{14,10},{7,3},{... | collective-permute-start | bytes 786440 | tf_op jit(solution)/shard_map/ppermute | solution.py:14
  150.2 18.2 %collective-permute-start.3 = (bf16[128,1024]{1,0:T(8,128)(2,1)S(1)}, bf16[128,1024]{1,0:T(8,128)(2,1)S(1)}, u32[]{:S(2)}, u32[]{:S(2)}) collective-permute-start(bf16[128,1024]{1,0:T(8,128)(2,1)S(1)} %fusion.58), channel_id=1, source_target_pairs={{0,4},{4,8},{8,12},{1,5},{5,9},{9,13},{2,6},{6,10},{10,14},{3,7},{... | collective-permute-start | bytes 786440 | tf_op jit(solution)/shard_map/ppermute | solution.py:14
  256.5 1.3 copy-start.1
  262.2 1.0 copy-start.2
  354.9 15.2 %collective-permute-start.6 = (f32[128,1024]{1,0:T(8,128)S(1)}, f32[128,1024]{1,0:T(8,128)S(1)}, u32[]{:S(2)}, u32[]{:S(2)}) collective-permute-start(f32[128,1024]{1,0:T(8,128)S(1)} %get-tuple-element.4), channel_id=1, source_target_pairs={{4,0},{8,4},{12,8},{5,1},{9,5},{13,9},{6,2},{10,6},{14,10},{7,3},{... | collective-permute-start | bytes 1572872 | tf_op jit(solution)/shard_map/ppermute | solution.py:14
  356.8 26.4 %collective-permute-start.8 = (f32[128,1024]{1,0:T(8,128)S(1)}, f32[128,1024]{1,0:T(8,128)S(1)}, u32[]{:S(2)}, u32[]{:S(2)}) collective-permute-start(f32[128,1024]{1,0:T(8,128)S(1)} %get-tuple-element.5), channel_id=1, source_target_pairs={{0,8},{4,12},{1,9},{5,13},{2,10},{6,14},{3,11},{7,15},{16,24},{20,... | collective-permute-start | bytes 1572872 | tf_op jit(solution)/shard_map/ppermute | solution.py:14
  359.6 33.0 %collective-permute-start.7 = (f32[128,1024]{1,0:T(8,128)S(1)}, f32[128,1024]{1,0:T(8,128)S(1)}, u32[]{:S(2)}, u32[]{:S(2)}) collective-permute-start(f32[128,1024]{1,0:T(8,128)S(1)} %get-tuple-element.6), channel_id=1, source_target_pairs={{0,4},{4,8},{8,12},{1,5},{5,9},{9,13},{2,6},{6,10},{10,14},{3,7},{... | collective-permute-start | bytes 1572872 | tf_op jit(solution)/shard_map/ppermute | solution.py:14
  393.6 12.0 %collective-permute-start.11 = (bf16[128,1024]{1,0:T(8,128)(2,1)S(1)}, bf16[128,1024]{1,0:T(8,128)(2,1)S(1)}, u32[]{:S(2)}, u32[]{:S(2)}) collective-permute-start(bf16[128,1024]{1,0:T(8,128)(2,1)S(1)} %get-tuple-element.2), channel_id=1, source_target_pairs={{8,0},{12,4},{9,1},{13,5},{10,2},{14,6},{11,3},{15,7},{24,16},{28,... | collective-permute-start | bytes 786440 | tf_op jit(solution)/shard_map/ppermute | solution.py:14
  394.9 18.4 %collective-permute-start.10 = (bf16[128,1024]{1,0:T(8,128)(2,1)S(1)}, bf16[128,1024]{1,0:T(8,128)(2,1)S(1)}, u32[]{:S(2)}, u32[]{:S(2)}) collective-permute-start(bf16[128,1024]{1,0:T(8,128)(2,1)S(1)} %get-tuple-element.2), channel_id=1, source_target_pairs={{4,0},{8,4},{12,8},{5,1},{9,5},{13,9},{6,2},{10,6},{14,10},{7,3},{... | collective-permute-start | bytes 786440 | tf_op jit(solution)/shard_map/ppermute | solution.py:14
  396.8 16.5 %collective-permute-start.9 = (bf16[128,1024]{1,0:T(8,128)(2,1)S(1)}, bf16[128,1024]{1,0:T(8,128)(2,1)S(1)}, u32[]{:S(2)}, u32[]{:S(2)}) collective-permute-start(bf16[128,1024]{1,0:T(8,128)(2,1)S(1)} %get-tuple-element.2), channel_id=1, source_target_pairs={{0,4},{4,8},{8,12},{1,5},{5,9},{9,13},{2,6},{6,10},{10,14},{3,7},{... | collective-permute-start | bytes 786440 | tf_op jit(solution)/shard_map/ppermute | solution.py:14
  501.6 1.2 copy-start.3
where the time goes:
time: 518 us; the launch traced here: 509 us
  matrix products  285 us (55%)
  waiting for transfers between devices  95.8 us (18%)
  starting transfers between devices  34.5 us (7%)
  other arithmetic  34 us (7%)
  blocking collectives  33.7 us (7%)
  local copies, waits for them, and re-layouts  23.6 us (5%)
    dot_general x2, matrix products, shards(): jnp.einsum('srf,ft->srt', lax.all_to_all(spread, ('rec', 'tr'), split_axi...  138 us
    dot_general x2, matrix products, shards(): jnp.einsum('srt,ft->srf', emitter_pieces, time_table, preferred_element_t...  127 us
    ppermute x12, waiting for transfers between devices, passed_along(): lax.ppermute(value, axis, [(source, source + steps) for source in range(f...  87.7 us
    unnamed x4, other arithmetic  31.1 us
    ppermute x12, starting transfers between devices, passed_along(): lax.ppermute(value, axis, [(source, source + steps) for source in range(f...  31 us
    all_to_all x2, blocking collectives, shards(): lax.all_to_all(spectra, ('rec', 'tr'), split_axis=2, concat_axis=1, tiled...  22.5 us
    dynamic_update_slice x2, local copies, waits for them, and re-layouts, shards(): buffer = lax.dynamic_update_slice_in_dim(buffer, shot_data[0], starts[0], 1)  12.2 us
    all_to_all x1, blocking collectives, shards(): lax.all_to_all(spread, ('rec', 'tr'), split_axis=1, concat_axis=2, tiled=...  11.2 us
  transfers between devices with their start and end apart: 13, of which 11 were waited for; matrix products, arithmetic and copies ran while one was open for 0% of the time, Pallas kernels for 0%

commit v1 on v0

--- a/solution.py
+++ b/solution.py
@@ -2,6 +2,8 @@
 
 import jax
 import jax.numpy as jnp
+import ml_dtypes
+import numpy as np
 from jax import lax
 from jax.sharding import PartitionSpec as P
 
@@ -15,13 +17,12 @@
 
 
 def cosine_table(order):
-    emitter_location = jnp.arange(order, dtype=jnp.int32)
-    phase = (2 * emitter_location[None, :] + 1) * emitter_location[:, None] % (4 * order)
-    table = jnp.cos(math.pi * phase.astype(jnp.float32) / (2.0 * order)) * math.sqrt(2.0 / order)
-    table = table * jnp.where(emitter_location[:, None] == 0, math.sqrt(0.5), 1.0).astype(
-        jnp.float32
-    )
-    return table.astype(jnp.bfloat16)
+    column = np.arange(order, dtype=np.int64)
+    phase = (2 * column[None, :] + 1) * column[:, None] % (4 * order)
+    table = np.cos(np.float32(math.pi) * phase.astype(np.float32) / np.float32(2.0 * order))
+    table = table * np.float32(math.sqrt(2.0 / order))
+    table = table * np.where(column[:, None] == 0, math.sqrt(0.5), 1.0).astype(np.float32)
+    return table.astype(ml_dtypes.bfloat16)
 
 
 def shards(model_init, record, activation_dither):
@@ -30,10 +31,10 @@
     time_len = freq_dev * lax.axis_size(("rec", "tr"))
     spacing = time_len // 2
     jitter = time_len // 4
-    hops = (time_len + jitter - spacing + window - 1) // window
+    hops = (time_len - 2) // window
     margin = (hops + 1) * window
-    time_table = cosine_table(time_len)
-    trace_table = cosine_table(traces)
+    time_table = jnp.asarray(cosine_table(time_len))
+    trace_table = jnp.asarray(cosine_table(traces))
     starts = jnp.arange(shots_dev, dtype=jnp.int32) * spacing + activation_dither - jitter + window
     width = window + margin
     model = model_init

time: 518 us -> 189 us (0.36)
  the two profiles are of different devices: /device:TPU:8 before, /device:TPU:1 now
where the time goes in v1:
time: 189 us; the launch traced here: 186 us
  waiting for transfers between devices  42.1 us (22%)
  starting transfers between devices  35.1 us (19%)
  other arithmetic  32 us (17%)
  matrix products  30.1 us (16%)
  blocking collectives  24.2 us (13%)
  local copies, waits for them, and re-layouts  21.3 us (11%)
    unnamed x4, other arithmetic  30.9 us
    ppermute x8, waiting for transfers between devices, passed_along(): lax.ppermute(value, axis, [(source, source + steps) for source in range(f...  27.4 us
    ppermute x8, starting transfers between devices, passed_along(): lax.ppermute(value, axis, [(source, source + steps) for source in range(f...  24.7 us
    all_to_all x1, blocking collectives, shards(): lax.all_to_all(spectra, ('rec', 'tr'), split_axis=2, concat_axis=1, tiled...  13.1 us
    dot_general x2, matrix products, shards(): jnp.einsum('srt,ft->srf', emitter_pieces, time_table, preferred_element_t...  12.7 us
    all_to_all x1, blocking collectives, shards(): lax.all_to_all(spread, ('rec', 'tr'), split_axis=1, concat_axis=2, tiled=...  11.1 us
    dot_general x2, matrix products, shards(): jnp.einsum('srf,ft->srt', lax.all_to_all(spread, ('rec', 'tr'), split_axi...  10.4 us
    dynamic_update_slice x2, local copies, waits for them, and re-layouts, shards(): buffer = lax.dynamic_update_slice_in_dim(buffer, shot_data[0], starts[0], 1)  7.95 us
  transfers between devices with their start and end apart: 10, of which 10 were waited for; matrix products, arithmetic and copies ran while one was open for 0% of the time, Pallas kernels for 0%

profile of v1, /device:TPU:1, one launch (start us, length us, event | category | flops | bytes accessed | tf_op | source)
XLA Modules:
  0.0 186.5 jit_solution(13262807480411533944)
XLA Ops:
  3.9 3.9 %reduce = bf16[512,512]{1,0:T(8,128)(2,1)S(1)} reduce(bf16[512,1,512]{2,1,0:T(2,128)(2,1)S(1)} %bitcast.67, bf16[]{:T(256)} %broadcast.29), dimensions={1}, to_apply=%bitcast.62.reduce_sub_computation | reduce | bytes 1048578
  8.9 4.3 %all-to-all-start = ((bf16[4,2,32768]{2,1,0:T(2,128)(2,1)}), bf16[4,2,32768]{2,1,0:T(2,128)(2,1)S(1)}, u32[]{:S(2)}, u32[]{:S(2)}) async-start(bf16[4,2,32768]{2,1,0:T(2,128)(2,1)} %reshape.64), calls=%async_computation | async-start | bytes 1048576 | tf_op jit(solution)/shard_map/all_to_all | solution.py:51
  13.9 7.1 %all-to-all-done = bf16[4,2,32768]{2,1,0:T(2,128)(2,1)S(1)} async-done(((bf16[4,2,32768]{2,1,0:T(2,128)(2,1)}), bf16[4,2,32768]{2,1,0:T(2,128)(2,1)S(1)}, u32[]{:S(2)}, u32[]{:S(2)}) %all-to-all-start) | async-done | bytes 524320 | tf_op jit(solution)/shard_map/all_to_all | solution.py:51
  21.9 4.7 %fusion.31 = f32[128,2048]{1,0:T(8,128)S(1)} fusion(bf16[128,2048]{0,1:T(8,128)(2,1)S(1)} %bitcast.71, bf16[2048,2048]{1,0:T(8,128)(2,1)} %constant.22.clone), kind=kOutput, calls=%fused_computation.45 | convolution fusion | flops 1073741824 | bytes 9961472 | tf_op jit(solution)/shard_map/srf,ft->srt/dot_general | solution.py:49
  26.8 2.7 %dynamic_update_slice.6 = f32[128,3072]{1,0:T(8,128)S(1)} dynamic-update-slice(f32[128,3072]{1,0:T(8,128)S(1)} %broadcast.19.clone, f32[128,2048]{1,0:T(8,128)S(1)} %fusion.31, s32[]{:T(128)} %constant.9.clone.1, s32[]{:T(128)S(6)} %select_n.2) | dynamic-update-slice | bytes 2097156 | tf_op jit(solution)/shard_map/dynamic_update_slice | solution.py:56
  30.9 4.9 %collective-permute-start.1 = (f32[128,1024]{1,0:T(8,128)S(1)}, f32[128,1024]{1,0:T(8,128)S(1)}, u32[]{:S(2)}, u32[]{:S(2)}) collective-permute-start(f32[128,1024]{1,0:T(8,128)S(1)} %get-tuple-element.15), channel_id=1, source_target_pairs={{0,4},{4,8},{8,12},{1,5},{5,9},{9,13},{2,6},{6,10},{10,14},{3,7},{... | collective-permute-start | bytes 1572872 | tf_op jit(solution)/shard_map/ppermute | solution.py:16
  35.8 9.3 %collective-permute-done = f32[128,1024]{1,0:T(8,128)S(1)} collective-permute-done((f32[128,1024]{1,0:T(8,128)S(1)}, f32[128,1024]{1,0:T(8,128)S(1)}, u32[]{:S(2)}, u32[]{:S(2)}) %collective-permute-start) | collective-permute-done | bytes 524320 | tf_op jit(solution)/shard_map/ppermute | solution.py:16
  47.6 4.9 %collective-permute-start.2 = (bf16[128,1024]{1,0:T(8,128)(2,1)S(1)}, bf16[128,1024]{1,0:T(8,128)(2,1)S(1)}, u32[]{:S(2)}, u32[]{:S(2)}) collective-permute-start(bf16[128,1024]{1,0:T(8,128)(2,1)S(1)} %fusion.18), channel_id=1, source_target_pairs={{0,4},{4,8},{8,12},{1,5},{5,9},{9,13},{2,6},{6,10},{10,14},{3,7},{... | collective-permute-start | bytes 786440 | tf_op jit(solution)/shard_map/ppermute | solution.py:16
  52.6 2.7 %collective-permute-done.3 = bf16[128,1024]{1,0:T(8,128)(2,1)S(1)} collective-permute-done((bf16[128,1024]{1,0:T(8,128)(2,1)S(1)}, bf16[128,1024]{1,0:T(8,128)(2,1)S(1)}, u32[]{:S(2)}, u32[]{:S(2)}) %collective-permute-start.3) | collective-permute-done | bytes 262176 | tf_op jit(solution)/shard_map/ppermute | solution.py:16
  56.2 6.4 %fusion = bf16[1,128,2048]{2,1,0:T(8,128)(2,1)S(1)} fusion(bf16[2048,2048]{1,0:T(8,128)(2,1)} %constant.22.clone, s32[]{:T(128)S(6)} %select_n.2, bf16[128,1024]{1,0:T(8,128)(2,1)S(1)} %collective-permute-done.2, bf16[128,1024]{1,0:T(8,128)(2,1)S(1)} %fusion.18, bf16[128,1024]{1,0:T(8,128)(2,1)S(1)} %collective-permute-done.3), kind=kOutput, calls=%fused_computation.2 | convolution fusion | flops 1075576832 | bytes 9699332 | tf_op jit(solution)/shard_map/srt,ft->srf/dot_general | solution.py:71
  63.3 11.6 %reduce.1 = bf16[2048,128]{1,0:T(8,128)(2,1)S(1)} reduce(bf16[2048,1,128]{2,1,0:T(2,128)(2,1)S(1)} %bitcast.69, bf16[]{:T(256)} %broadcast.29), dimensions={1}, to_apply=%bitcast.43.reduce_sub_computation | reduce | bytes 1048578
  75.8 6.1 %all-to-all-start.1 = ((bf16[4,2,32768]{2,1,0:T(2,128)(2,1)}), bf16[4,2,32768]{2,1,0:T(2,128)(2,1)S(1)}, u32[]{:S(2)}, u32[]{:S(2)}) async-start(bf16[4,2,32768]{2,1,0:T(2,128)(2,1)} %reshape.66), calls=%async_computation.1 | async-start | bytes 1048576 | tf_op jit(solution)/shard_map/all_to_all | solution.py:76
  82.3 7.6 %all-to-all-done.1 = bf16[4,2,32768]{2,1,0:T(2,128)(2,1)S(1)} async-done(((bf16[4,2,32768]{2,1,0:T(2,128)(2,1)}), bf16[4,2,32768]{2,1,0:T(2,128)(2,1)S(1)}, u32[]{:S(2)}, u32[]{:S(2)}) %all-to-all-start.1) | async-done | bytes 524320 | tf_op jit(solution)/shard_map/all_to_all | solution.py:76
  95.7 3.9 %reduce.2 = bf16[512,512]{1,0:T(8,128)(2,1)S(1)} reduce(bf16[512,1,512]{2,1,0:T(2,128)(2,1)S(1)} %bitcast.70, bf16[]{:T(256)} %broadcast.29), dimensions={1}, to_apply=%bitcast.45.reduce_sub_computation | reduce | bytes 1048578
  99.9 11.1 %all_to_all.60 = bf16[4,2,32768]{2,1,0:T(2,128)(2,1)S(1)} all-to-all(bf16[4,2,32768]{2,1,0:T(2,128)(2,1)S(1)} %reshape.68), channel_id=1, replica_groups=mesh['swath'=2,'shot'=4,'rec'=2,'tr'=2] {'rec','tr'}, dimensions={0} | all-to-all | bytes 1048576 | tf_op jit(solution)/shard_map/all_to_all | solution.py:51
  111.9 5.7 %fusion.32 = f32[128,2048]{1,0:T(8,128)} fusion(bf16[128,2048]{0,1:T(8,128)(2,1)S(1)} %bitcast.72, bf16[2048,2048]{1,0:T(8,128)(2,1)} %constant.22.clone), kind=kOutput, calls=%fused_computation.46 | convolution fusion | flops 1073741824 | bytes 9961472 | tf_op jit(solution)/shard_map/srf,ft->srt/dot_general | solution.py:49
  117.8 5.2 %dynamic_update_slice.7 = f32[128,3072]{1,0:T(8,128)S(1)} dynamic-update-slice(f32[128,3072]{1,0:T(8,128)S(1)} %broadcast.19, f32[128,2048]{1,0:T(8,128)} %fusion.32, s32[]{:T(128)} %constant.9.clone.1, s32[]{:T(128)S(6)} %select_n.2) | dynamic-update-slice | bytes 2097156 | tf_op jit(solution)/shard_map/dynamic_update_slice | solution.py:56
  124.4 4.8 %collective-permute-start.5 = (f32[128,1024]{1,0:T(8,128)S(1)}, f32[128,1024]{1,0:T(8,128)S(1)}, u32[]{:S(2)}, u32[]{:S(2)}) collective-permute-start(f32[128,1024]{1,0:T(8,128)S(1)} %get-tuple-element.13), channel_id=1, source_target_pairs={{0,4},{4,8},{8,12},{1,5},{5,9},{9,13},{2,6},{6,10},{10,14},{3,7},{... | collective-permute-start | bytes 1572872 | tf_op jit(solution)/shard_map/ppermute | solution.py:16
  129.2 9.2 %collective-permute-done.4 = f32[128,1024]{1,0:T(8,128)S(1)} collective-permute-done((f32[128,1024]{1,0:T(8,128)S(1)}, f32[128,1024]{1,0:T(8,128)S(1)}, u32[]{:S(2)}, u32[]{:S(2)}) %collective-permute-start.4) | collective-permute-done | bytes 524320 | tf_op jit(solution)/shard_map/ppermute | solution.py:16
  141.5 5.0 %collective-permute-start.6 = (bf16[128,1024]{1,0:T(8,128)(2,1)S(1)}, bf16[128,1024]{1,0:T(8,128)(2,1)S(1)}, u32[]{:S(2)}, u32[]{:S(2)}) collective-permute-start(bf16[128,1024]{1,0:T(8,128)(2,1)S(1)} %get-tuple-element.10), channel_id=1, source_target_pairs={{0,4},{4,8},{8,12},{1,5},{5,9},{9,13},{2,6},{6,10},{10,14},{3,7},{... | collective-permute-start | bytes 786440 | tf_op jit(solution)/shard_map/ppermute | solution.py:16
  146.6 2.4 %collective-permute-done.7 = bf16[128,1024]{1,0:T(8,128)(2,1)S(1)} collective-permute-done((bf16[128,1024]{1,0:T(8,128)(2,1)S(1)}, bf16[128,1024]{1,0:T(8,128)(2,1)S(1)}, u32[]{:S(2)}, u32[]{:S(2)}) %collective-permute-start.7) | collective-permute-done | bytes 262176 | tf_op jit(solution)/shard_map/ppermute | solution.py:16
  149.9 6.4 %fusion.1 = bf16[1,128,2048]{2,1,0:T(8,128)(2,1)S(1)} fusion(bf16[2048,2048]{1,0:T(8,128)(2,1)} %constant.22.clone, s32[]{:T(128)S(6)} %select_n.2, bf16[128,1024]{1,0:T(8,128)(2,1)S(1)} %collective-permute-done.6, bf16[128,1024]{1,0:T(8,128)(2,1)S(1)} %get-tuple-element.10, bf16[128,1024]{1,0:T(8,128)(2,1)S(1)} %collective-permute-done.7), kind=kOutput, calls=%fused_computation.3 | convolution fusion | flops 1075576832 | bytes 9699332 | tf_op jit(solution)/shard_map/srt,ft->srf/dot_general | solution.py:71
  157.0 11.6 %reduce.3 = bf16[2048,128]{1,0:T(8,128)(2,1)S(1)} reduce(bf16[2048,1,128]{2,1,0:T(2,128)(2,1)S(1)} %bitcast.68, bf16[]{:T(256)} %broadcast.29), dimensions={1}, to_apply=%bitcast.47.reduce_sub_computation | reduce | bytes 1048578
  168.7 13.1 %all_to_all.61 = bf16[4,2,32768]{2,1,0:T(2,128)(2,1)S(1)} all-to-all(bf16[4,2,32768]{2,1,0:T(2,128)(2,1)S(1)} %reshape.70), channel_id=1, replica_groups=mesh['swath'=2,'shot'=4,'rec'=2,'tr'=2] {'rec','tr'}, dimensions={0} | all-to-all | bytes 1048576 | tf_op jit(solution)/shard_map/all_to_all | solution.py:76
  (47 shorter events, 30.3 us)
Async XLA Ops:
  8.9 12.1 %all-to-all-start = ((bf16[4,2,32768]{2,1,0:T(2,128)(2,1)}), bf16[4,2,32768]{2,1,0:T(2,128)(2,1)S(1)}, u32[]{:S(2)}, u32[]{:S(2)}) async-start(bf16[4,2,32768]{2,1,0:T(2,128)(2,1)} %reshape.64), calls=%async_computation | async-start | bytes 1048576 | tf_op jit(solution)/shard_map/all_to_all | solution.py:51
  21.9 24.2 %copy-start.1 = (f32[128,1024]{1,0:T(8,128)S(1)}, f32[128,1024]{1,0:T(8,128)}, u32[]{:S(2)}) copy-start(f32[128,1024]{1,0:T(8,128)} %param.6) | copy-start | bytes 1572868
  29.6 15.5 %collective-permute-start = (f32[128,1024]{1,0:T(8,128)S(1)}, f32[128,1024]{1,0:T(8,128)S(1)}, u32[]{:S(2)}, u32[]{:S(2)}) collective-permute-start(f32[128,1024]{1,0:T(8,128)S(1)} %get-tuple-element.14), channel_id=1, source_target_pairs={{4,0},{8,4},{12,8},{5,1},{9,5},{13,9},{6,2},{10,6},{14,10},{7,3},{... | collective-permute-start | bytes 1572872 | tf_op jit(solution)/shard_map/ppermute | solution.py:16
  30.9 51.0 %copy-start = (f32[1,512,512]{2,1,0:T(8,128)S(1)}, f32[1,512,512]{2,1,0:T(8,128)}, u32[]{:S(2)}) copy-start(f32[1,512,512]{2,1,0:T(8,128)} %param.5) | copy-start | bytes 3145732
  30.9 15.2 %collective-permute-start.1 = (f32[128,1024]{1,0:T(8,128)S(1)}, f32[128,1024]{1,0:T(8,128)S(1)}, u32[]{:S(2)}, u32[]{:S(2)}) collective-permute-start(f32[128,1024]{1,0:T(8,128)S(1)} %get-tuple-element.15), channel_id=1, source_target_pairs={{0,4},{4,8},{8,12},{1,5},{5,9},{9,13},{2,6},{6,10},{10,14},{3,7},{... | collective-permute-start | bytes 1572872 | tf_op jit(solution)/shard_map/ppermute | solution.py:16
  46.3 8.9 %collective-permute-start.3 = (bf16[128,1024]{1,0:T(8,128)(2,1)S(1)}, bf16[128,1024]{1,0:T(8,128)(2,1)S(1)}, u32[]{:S(2)}, u32[]{:S(2)}) collective-permute-start(bf16[128,1024]{1,0:T(8,128)(2,1)S(1)} %fusion.18), channel_id=1, source_target_pairs={{4,0},{8,4},{12,8},{5,1},{9,5},{13,9},{6,2},{10,6},{14,10},{7,3},{... | collective-permute-start | bytes 786440 | tf_op jit(solution)/shard_map/ppermute | solution.py:16
  47.6 8.6 %collective-permute-start.2 = (bf16[128,1024]{1,0:T(8,128)(2,1)S(1)}, bf16[128,1024]{1,0:T(8,128)(2,1)S(1)}, u32[]{:S(2)}, u32[]{:S(2)}) collective-permute-start(bf16[128,1024]{1,0:T(8,128)(2,1)S(1)} %fusion.18), channel_id=1, source_target_pairs={{0,4},{4,8},{8,12},{1,5},{5,9},{9,13},{2,6},{6,10},{10,14},{3,7},{... | collective-permute-start | bytes 786440 | tf_op jit(solution)/shard_map/ppermute | solution.py:16
  75.8 14.1 %all-to-all-start.1 = ((bf16[4,2,32768]{2,1,0:T(2,128)(2,1)}), bf16[4,2,32768]{2,1,0:T(2,128)(2,1)S(1)}, u32[]{:S(2)}, u32[]{:S(2)}) async-start(bf16[4,2,32768]{2,1,0:T(2,128)(2,1)} %reshape.66), calls=%async_computation.1 | async-start | bytes 1048576 | tf_op jit(solution)/shard_map/all_to_all | solution.py:76
  111.9 27.4 %copy-start.2 = (f32[128,1024]{1,0:T(8,128)S(1)}, f32[128,1024]{1,0:T(8,128)}, u32[]{:S(2)}) copy-start(f32[128,1024]{1,0:T(8,128)} %param.6) | copy-start | bytes 1572868
  123.1 15.3 %collective-permute-start.4 = (f32[128,1024]{1,0:T(8,128)S(1)}, f32[128,1024]{1,0:T(8,128)S(1)}, u32[]{:S(2)}, u32[]{:S(2)}) collective-permute-start(f32[128,1024]{1,0:T(8,128)S(1)} %get-tuple-element.12), channel_id=1, source_target_pairs={{4,0},{8,4},{12,8},{5,1},{9,5},{13,9},{6,2},{10,6},{14,10},{7,3},{... | collective-permute-start | bytes 1572872 | tf_op jit(solution)/shard_map/ppermute | solution.py:16
  124.4 14.9 %collective-permute-start.5 = (f32[128,1024]{1,0:T(8,128)S(1)}, f32[128,1024]{1,0:T(8,128)S(1)}, u32[]{:S(2)}, u32[]{:S(2)}) collective-permute-start(f32[128,1024]{1,0:T(8,128)S(1)} %get-tuple-element.13), channel_id=1, source_target_pairs={{0,4},{4,8},{8,12},{1,5},{5,9},{9,13},{2,6},{6,10},{10,14},{3,7},{... | collective-permute-start | bytes 1572872 | tf_op jit(solution)/shard_map/ppermute | solution.py:16
  140.3 8.7 %collective-permute-start.7 = (bf16[128,1024]{1,0:T(8,128)(2,1)S(1)}, bf16[128,1024]{1,0:T(8,128)(2,1)S(1)}, u32[]{:S(2)}, u32[]{:S(2)}) collective-permute-start(bf16[128,1024]{1,0:T(8,128)(2,1)S(1)} %get-tuple-element.10), channel_id=1, source_target_pairs={{4,0},{8,4},{12,8},{5,1},{9,5},{13,9},{6,2},{10,6},{14,10},{7,3},{... | collective-permute-start | bytes 786440 | tf_op jit(solution)/shard_map/ppermute | solution.py:16
  141.5 8.3 %collective-permute-start.6 = (bf16[128,1024]{1,0:T(8,128)(2,1)S(1)}, bf16[128,1024]{1,0:T(8,128)(2,1)S(1)}, u32[]{:S(2)}, u32[]{:S(2)}) collective-permute-start(bf16[128,1024]{1,0:T(8,128)(2,1)S(1)} %get-tuple-element.10), channel_id=1, source_target_pairs={{0,4},{4,8},{8,12},{1,5},{5,9},{9,13},{2,6},{6,10},{10,14},{3,7},{... | collective-permute-start | bytes 786440 | tf_op jit(solution)/shard_map/ppermute | solution.py:16

commit v2 on v1

v2 whole, which is shorter than its diff:
```python
import functools
import math

import jax
import jax.numpy as jnp
import ml_dtypes
import numpy as np
from jax import lax
from jax.experimental import pallas as pl
from jax.experimental.pallas import tpu as pltpu
from jax.sharding import PartitionSpec as P

ITERS = 2
CHUNK = 32
TILE = 512
BF = jnp.bfloat16
F32 = jnp.float32


def cosine_table(order):
    column = np.arange(order, dtype=np.int64)
    phase = (2 * column[None, :] + 1) * column[:, None] % (4 * order)
    table = np.cos(np.float32(math.pi) * phase.astype(np.float32) / np.float32(2.0 * order))
    table = table * np.float32(math.sqrt(2.0 / order))
    table = table * np.where(column[:, None] == 0, math.sqrt(0.5), 1.0).astype(np.float32)
    return table.astype(ml_dtypes.bfloat16)


def dot(a, b):
    return jnp.dot(a, b, preferred_element_type=F32)


def kernel(
    sizes, dither, model_in, record, trace_table, trace_table_t, time_hbm, time_t_hbm,
    model, residual,
    time_table, time_table_t, narrow_model, spread_out, spread_in, shot_sum, up_out, down_out,
    up_in, down_in, narrow, tail_in, head_in, windows, spectra_out, spectra_in,
    table_sem, spread_send, spread_recv, part_send, part_recv, res_send, res_recv,
    spectra_send, spectra_recv,
):
    recs, cores, shots, time_len, freqs, traces, window = sizes
    jitter = time_len // 4
    span = time_len + jitter
    high = jitter + window
    rec, core, shot = lax.axis_index("rec"), lax.axis_index("tr"), lax.axis_index("shot")
    me = rec * cores + core
    offsets = [(a, b) for a in range(1, recs) for b in range(cores)]
    offsets += [(0, b) for b in range(1, cores)]
    has_before, has_after = shot > 0, shot < shots - 1

    def peer(a, b):
        return lax.rem(rec + a, recs), lax.rem(core + b, cores)

    def origin(a, b):
        return lax.rem(rec + recs - a, recs), lax.rem(core + cores - b, cores)

    def rows_of(index, size):
        return pl.ds(pl.multiple_of(index * size, size), size)

    copy_a = pltpu.make_async_copy(time_hbm, time_table, table_sem.at[0])
    copy_b = pltpu.make_async_copy(time_t_hbm, time_table_t, table_sem.at[1])
    copy_a.start()
    copy_b.start()

    barrier = pltpu.get_barrier_semaphore()
    for a, b in offsets:
        to_rec, to_core = peer(a, b)
        pl.semaphore_signal(barrier, inc=1, device_id={"rec": to_rec, "tr": to_core})

    @pl.when(has_before)
    def _():
        pl.semaphore_signal(barrier, inc=1, device_id={"shot": shot - 1})

    @pl.when(has_after)
    def _():
        pl.semaphore_signal(barrier, inc=1, device_id={"shot": shot + 1})

    model[...] = model_in[...]
    narrow_model[...] = model_in[...].astype(BF)

    @pl.when(jnp.logical_not(has_before))
    def _():
        tail_in[...] = jnp.zeros_like(tail_in)

    @pl.when(jnp.logical_not(has_after))
    def _():
        head_in[...] = jnp.zeros_like(head_in)

    beside = has_before.astype(jnp.int32) + has_after.astype(jnp.int32)
    pl.semaphore_wait(barrier, len(offsets) + beside)

    delay = dither[0]
    back = jnp.where(delay == 0, 0, span - delay)

    def spread_copy(it, j, slot):
        to_rec, to_core = peer(*offsets[j])
        return pltpu.make_async_remote_copy(
            spread_out.at[it, j], spread_in.at[it, slot], spread_send.at[it, j],
            spread_recv.at[it, j], device_id={"rec": to_rec, "tr": to_core},
        )

    def spectra_copy(it, j, slot):
        to_rec, to_core = peer(*offsets[j])
        return pltpu.make_async_remote_copy(
            spectra_out.at[it, j], spectra_in.at[it, rows_of(slot, traces)],
            spectra_send.at[it, j], spectra_recv.at[it, j],
            device_id={"rec": to_rec, "tr": to_core},
        )

    def up_copy(it, c):
        rows = pl.ds(c * CHUNK, CHUNK)
        return pltpu.make_async_remote_copy(
            up_out.at[it, rows], up_in.at[it, rows], part_send.at[it, 0, c],
            part_recv.at[it, 0, c], device_id={"shot": shot + 1},
        )

    def down_copy(it, c):
        rows = pl.ds(c * CHUNK, CHUNK)
        return pltpu.make_async_remote_copy(
            down_out.at[it, rows], down_in.at[it, rows], part_send.at[it, 1, c],
            part_recv.at[it, 1, c], device_id={"shot": shot - 1},
        )

    def tail_copy(it, c):
        rows = pl.ds(c * CHUNK, CHUNK)
        return pltpu.make_async_remote_copy(
            narrow.at[it, rows, pl.ds(window - jitter, jitter)], tail_in.at[it, rows],
            res_send.at[it, 0, c], res_recv.at[it, 0, c], device_id={"shot": shot + 1},
        )

    def head_copy(it, c):
        rows = pl.ds(c * CHUNK, CHUNK)
        return pltpu.make_async_remote_copy(
            narrow.at[it, rows], head_in.at[it, rows],
            res_send.at[it, 1, c], res_recv.at[it, 1, c], device_id={"shot": shot - 1},
        )

    chunks = traces // CHUNK
    for it in range(ITERS):
        for j, (a, b) in enumerate(offsets):
            to_rec, to_core = peer(a, b)
            block = dot(trace_table_t[rows_of(to_rec * cores + to_core, traces), :], narrow_model[...])
            spread_out[it, j] = block.astype(BF)
            spread_copy(it, j, me).start()
        spread_in[it, me] = dot(trace_table_t[rows_of(me, traces), :], narrow_model[...]).astype(BF)
        if it == 0:
            copy_a.wait()

        def add_block(slot, first):
            @pl.loop(0, time_len // TILE)
            def _(i):
                columns = pl.ds(pl.multiple_of(i * TILE, TILE), TILE)
                term = dot(spread_in[it, slot], time_table[rows_of(slot, freqs), columns])
                if first:
                    shot_sum[:, columns] = term
                else:
                    shot_sum[:, columns] += term

        add_block(me, True)
        for j in list(range(len(offsets)))[::-1][: cores - 1] + list(range(len(offsets)))[: -(cores - 1)]:
            from_rec, from_core = origin(*offsets[j])
            slot = from_rec * cores + from_core
            spread_copy(it, j, slot).wait_recv()
            add_block(slot, False)

        for c in range(chunks):
            rows = pl.ds(c * CHUNK, CHUNK)
            data = jnp.concatenate([shot_sum[rows, :], jnp.zeros((CHUNK, jitter), F32)], axis=1)
            data = pltpu.roll(data, delay, 1)
            up_out[it, rows, :] = data[:, high:].astype(BF)
            down_out[it, rows, :] = data[:, :jitter].astype(BF)
            residual[rows, :] = record[rows, :] - data[:, jitter:high]

            @pl.when(has_after)
            def _():
                up_copy(it, c).start()

            @pl.when(has_before)
            def _():
                down_copy(it, c).start()

        for c in range(chunks):
            rows = pl.ds(c * CHUNK, CHUNK)

            @pl.when(has_before)
            def _():
                up_copy(it, c).wait_recv()
                residual[rows, :] -= up_in[it, rows, :].astype(F32)

            @pl.when(has_after)
            def _():
                down_copy(it, c).wait_recv()
                residual[rows, pl.ds(window - jitter, jitter)] -= down_in[it, rows, :].astype(F32)

            narrow[it, rows, :] = residual[rows, :].astype(BF)

            @pl.when(has_before)
            def _():
                head_copy(it, c).start()

            @pl.when(has_after)
            def _():
                tail_copy(it, c).start()

        for c in range(chunks):
            rows = pl.ds(c * CHUNK, CHUNK)

            @pl.when(has_before)
            def _():
                tail_copy(it, c).wait_recv()

            @pl.when(has_after)
            def _():
                head_copy(it, c).wait_recv()

            data = jnp.concatenate(
                [tail_in[it, rows, :], narrow[it, rows, :], head_in[it, rows, :]], axis=1
            ).astype(F32)
            windows[rows, :] = pltpu.roll(data, back, 1)[:, :time_len].astype(BF)

        if it == 0:
            copy_b.wait()
        for j, (a, b) in enumerate(offsets):
            to_rec, to_core = peer(a, b)
            columns = rows_of(to_rec * cores + to_core, freqs)
            spectra_out[it, j] = dot(windows[...], time_table_t[:, columns]).astype(BF)
            spectra_copy(it, j, me).start()
        spectra_in[it, rows_of(me, traces)] = dot(
            windows[...], time_table_t[:, rows_of(me, freqs)]
        ).astype(BF)

        for a in range(recs):
            for j, (far, _b) in enumerate(offsets):
                if far == a:
                    from_rec, from_core = origin(*offsets[j])
                    spectra_copy(it, j, from_rec * cores + from_core).wait_recv()
            part = rows_of(lax.rem(rec + recs - a, recs), cores * traces)
            last = a == recs - 1

            @pl.loop(0, model.shape[0] // 128)
            def _(i):
                out_rows = pl.ds(pl.multiple_of(i * 128, 128), 128)
                grad = dot(trace_table[out_rows, part], spectra_in[it, part])
                value = model[out_rows, :] + 0.5 * grad
                if last:
                    value = value - jnp.clip(value, -0.3, 0.3)
                    narrow_model[out_rows, :] = value.astype(BF)
                model[out_rows, :] = value

    for it in range(ITERS):
        for j in range(len(offsets)):
            spread_copy(it, j, me).wait_send()
            spectra_copy(it, j, me).wait_send()
        for c in range(chunks):

            @pl.when(has_after)
            def _():
                up_copy(it, c).wait_send()
                tail_copy(it, c).wait_send()

            @pl.when(has_before)
            def _():
                down_copy(it, c).wait_send()
                head_copy(it, c).wait_send()


def shards(model_init, record, activation_dither):
    _, waves, freqs = model_init.shape
    traces, window = record.shape
    recs, cores, shots = lax.axis_size("rec"), lax.axis_size("tr"), lax.axis_size("shot")
    group = recs * cores
    time_len = freqs * group
    jitter = time_len // 4
    time_table, trace_table = cosine_table(time_len), cosine_table(waves)
    chunks = traces // CHUNK
    vmem, hbm = pl.BlockSpec(memory_space=pltpu.VMEM), pl.BlockSpec(memory_space=pl.ANY)
    dma = pltpu.SemaphoreType.DMA
    model, residual = pl.pallas_call(
        functools.partial(kernel, (recs, cores, shots, time_len, freqs, traces, window)),
        out_shape=[
            jax.ShapeDtypeStruct((waves, freqs), F32),
            jax.ShapeDtypeStruct((traces, window), F32),
        ],
        in_specs=[pl.BlockSpec(memory_space=pltpu.SMEM)] + [vmem] * 4 + [hbm] * 2,
        out_specs=[vmem, vmem],
        scratch_shapes=[
            pltpu.VMEM((time_len, time_len), BF),
            pltpu.VMEM((time_len, time_len), BF),
            pltpu.VMEM((waves, freqs), BF),
            pltpu.VMEM((ITERS, group - 1, traces, freqs), BF),
            pltpu.VMEM((ITERS, group, traces, freqs), BF),
            pltpu.VMEM((traces, time_len), F32),
            pltpu.VMEM((ITERS, traces, time_len - window), BF),
            pltpu.VMEM((ITERS, traces, jitter), BF),
            pltpu.VMEM((ITERS, traces, time_len - window), BF),
            pltpu.VMEM((ITERS, traces, jitter), BF),
            pltpu.VMEM((ITERS, traces, window), BF),
            pltpu.VMEM((ITERS, traces, jitter), BF),
            pltpu.VMEM((ITERS, traces, window), BF),
            pltpu.VMEM((traces, time_len), BF),
            pltpu.VMEM((ITERS, group - 1, traces, freqs), BF),
            pltpu.VMEM((ITERS, group * traces, freqs), BF),
            dma((2,)),
            dma((ITERS, group - 1)),
            dma((ITERS, group - 1)),
            dma((ITERS, 2, chunks)),
            dma((ITERS, 2, chunks)),
            dma((ITERS, 2, chunks)),
            dma((ITERS, 2, chunks)),
            dma((ITERS, group - 1)),
            dma((ITERS, group - 1)),
        ],
        compiler_params=pltpu.CompilerParams(
            collective_id=0, has_side_effects=True, vmem_limit_bytes=48 * 1024 * 1024
        ),
        name="deblend",
    )(
        activation_dither, model_init[0], record, jnp.asarray(trace_table),
        jnp.asarray(np.ascontiguousarray(trace_table.T)), jnp.asarray(time_table),
        jnp.asarray(np.ascontiguousarray(time_table.T)),
    )
    return model[None], residual


def solution(mesh):
    return jax.shard_map(
        shards,
        mesh=mesh,
        in_specs=(
            P(("swath", "shot"), None, ("rec", "tr")),
            P(("rec", "tr"), ("swath", "shot")),
            P(("swath", "shot")),
        ),
        out_specs=(P(("swath", "shot"), None, ("rec", "tr")), P(("rec", "tr"), ("swath", "shot"))),
        check_vma=False,
    )
```

time: 189 us -> 65.7 us (0.35); the launches traced: 186 us -> 65.4 us
  Pallas kernels: 0 us -> 58 us
  waiting for transfers between devices: 42.1 us -> 0 us
  starting transfers between devices: 35.1 us -> 0 us
  other arithmetic: 32 us -> 0 us
  matrix products: 30.1 us -> 0 us
  blocking collectives: 24.2 us -> 0 us
  local copies, waits for them, and re-layouts: 21.3 us -> 6.11 us
    pallas_call x0 -> x1, Pallas kernels: none -> 58 us  [shards(): pl.pallas_call(functools.partial(kernel, (recs, cores, shots, time_len, f...]
    unnamed x4 -> x0, other arithmetic: 30.9 us -> none
    dot_general x8 -> x0, matrix products: 30.1 us -> none  [the longest x2 12.7 us: shards(): jnp.einsum('srt,ft->srf', emitter_pieces, time_table, preferred_element_t...]
    ppermute x8 -> x0, waiting for transfers between devices: 27.4 us -> none  [passed_along(): lax.ppermute(value, axis, [(source, source + steps) for source in range(f...]
    ppermute x8 -> x0, starting transfers between devices: 24.7 us -> none  [passed_along(): lax.ppermute(value, axis, [(source, source + steps) for source in range(f...]
    all_to_all x2 -> x0, blocking collectives: 24.2 us -> none  [the longest x1 13.1 us: shards(): lax.all_to_all(spectra, ('rec', 'tr'), split_axis=2, concat_axis=1, tiled...]
    all_to_all x2 -> x0, waiting for transfers between devices: 14.8 us -> none  [the longest x1 7.64 us: shards(): lax.all_to_all(spectra, ('rec', 'tr'), split_axis=2, concat_axis=1, tiled...]
    all_to_all x2 -> x0, starting transfers between devices: 10.4 us -> none  [the longest x1 6.13 us: shards(): lax.all_to_all(spectra, ('rec', 'tr'), split_axis=2, concat_axis=1, tiled...]
  transfers between devices with their start and end apart: 10 -> 0, of which waited for: 10 -> 0; matrix products, arithmetic and copies ran while one was open for 0% -> 0% of each run, Pallas kernels for 0% -> 0%
where the time goes in v2:
time: 65.7 us; the launch traced here: 65.4 us
  Pallas kernels  58 us (88%)
  local copies, waits for them, and re-layouts  6.11 us (9%)
  between operations  1.3 us (2%)
    pallas_call x1, Pallas kernels, shards(): pl.pallas_call(functools.partial(kernel, (recs, cores, shots, time_len, f...  58 us
    unnamed x10, local copies, waits for them, and re-layouts  6.11 us

profile of v2, /device:TPU:1, one launch (start us, length us, event | category | flops | bytes accessed | tf_op | source)
XLA Modules:
  0.0 65.4 jit_solution(12895870276999401649)
XLA Ops:
  1.3 0.0 copy-start
  1.3 1.2 %copy-done = f32[1,512,512]{2,1,0:T(8,128)S(1)} copy-done((f32[1,512,512]{2,1,0:T(8,128)S(1)}, f32[1,512,512]{2,1,0:T(8,128)}, u32[]{:S(2)}) %copy-start) | copy-done | bytes 1048600
  2.5 0.0 copy-start.1
  2.5 1.0 %copy-done.1 = f32[128,1024]{1,0:T(8,128)S(1)} copy-done((f32[128,1024]{1,0:T(8,128)S(1)}, f32[128,1024]{1,0:T(8,128)}, u32[]{:S(2)}) %copy-start.1) | copy-done | bytes 524312
  3.5 0.0 copy-start.2
  3.5 1.0 %copy-done.2 = bf16[512,512]{1,0:T(8,128)(2,1)S(1)} copy-done((bf16[512,512]{1,0:T(8,128)(2,1)S(1)}, bf16[512,512]{1,0:T(8,128)(2,1)}, u32[]{:S(2)}) %copy-start.2) | copy-done | bytes 524312
  4.6 0.0 copy-start.3
  4.6 1.0 %copy-done.3 = bf16[512,512]{1,0:T(8,128)(2,1)S(1)} copy-done((bf16[512,512]{1,0:T(8,128)(2,1)S(1)}, bf16[512,512]{1,0:T(8,128)(2,1)}, u32[]{:S(2)}) %copy-start.3) | copy-done | bytes 524312
  5.6 58.0 %deblend.1 = (f32[512,512]{1,0:T(8,128)S(1)}, f32[128,1024]{1,0:T(8,128)S(1)}) custom-call(s32[1]{0:T(128)S(6)} %copy.11.dither, f32[512,512]{1,0:T(8,128)S(1)} %bitcast.2, f32[128,1024]{1,0:T(8,128)S(1)} %copy-done.1, bf16[512,512]{1,0:T(8,128)(2,1)S(1)} %copy-done.3, bf16[512,512]{1,0:T(8,128)(2,1)S(1)} %copy-done.2, ...), custom_call_target="tpu_custom_call" | custom-call | tf_op jit(solution)/shard_map/deblend/pallas_call | solution.py:278
  63.6 1.0 %copy.12 = f32[1,512,512]{2,1,0:T(8,128)} copy(f32[1,512,512]{2,1,0:T(8,128)S(1)} %bitcast.3) | data formatting | bytes 2097152
  64.6 0.8 %copy.13 = f32[128,1024]{1,0:T(8,128)} copy(f32[128,1024]{1,0:T(8,128)S(1)} %get-tuple-element.9) | data formatting | bytes 1048576
Async XLA Ops:
  1.3 1.2 %copy-start = (f32[1,512,512]{2,1,0:T(8,128)S(1)}, f32[1,512,512]{2,1,0:T(8,128)}, u32[]{:S(2)}) copy-start(f32[1,512,512]{2,1,0:T(8,128)} %param.7) | copy-start | bytes 3145732
  2.5 1.0 %copy-start.1 = (f32[128,1024]{1,0:T(8,128)S(1)}, f32[128,1024]{1,0:T(8,128)}, u32[]{:S(2)}) copy-start(f32[128,1024]{1,0:T(8,128)} %record.1) | copy-start | bytes 1572868
  3.5 1.0 %copy-start.2 = (bf16[512,512]{1,0:T(8,128)(2,1)S(1)}, bf16[512,512]{1,0:T(8,128)(2,1)}, u32[]{:S(2)}) copy-start(bf16[512,512]{1,0:T(8,128)(2,1)} %constant.9.clone.trace_table_t) | copy-start | bytes 1572868
  4.6 1.0 %copy-start.3 = (bf16[512,512]{1,0:T(8,128)(2,1)S(1)}, bf16[512,512]{1,0:T(8,128)(2,1)}, u32[]{:S(2)}) copy-start(bf16[512,512]{1,0:T(8,128)(2,1)} %constant.8.clone.trace_table) | copy-start | bytes 1572868

commit v3 on v2

v3 whole, which is shorter than its diff:
```python
import functools
import math

import jax
import jax.numpy as jnp
import ml_dtypes
import numpy as np
from jax import lax
from jax.experimental import pallas as pl
from jax.experimental.pallas import tpu as pltpu
from jax.sharding import PartitionSpec as P

ITERS = 2
PARTS = 2
TILE = 1024
BF = jnp.bfloat16
F32 = jnp.float32


def cosine_table(order):
    column = np.arange(order, dtype=np.int64)
    phase = (2 * column[None, :] + 1) * column[:, None] % (4 * order)
    table = np.cos(np.float32(math.pi) * phase.astype(np.float32) / np.float32(2.0 * order))
    table = table * np.float32(math.sqrt(2.0 / order))
    table = table * np.where(column[:, None] == 0, math.sqrt(0.5), 1.0).astype(np.float32)
    return table.astype(ml_dtypes.bfloat16)


def dot(a, b):
    return jnp.dot(a, b, preferred_element_type=F32)


def kernel(
    sizes, dither, model_hbm, record_hbm, trace_hbm, trace_t_hbm, time_hbm, time_t_hbm,
    model, residual,
    record, trace_table, trace_table_t, time_table, time_table_t, narrow_model, spread_out, spread_in, shot_sum, up_out, down_out,
    up_in, down_in, narrow, tail_in, head_in, windows, spectra_out, spectra_in,
    table_sem, spread_send, spread_recv, part_send, part_recv, res_send, res_recv,
    spectra_send, spectra_recv,
):
    recs, cores, shots, time_len, freqs, traces, window = sizes
    jitter = time_len // 4
    span = time_len + jitter
    high = jitter + window
    rec, core, shot = lax.axis_index("rec"), lax.axis_index("tr"), lax.axis_index("shot")
    me = rec * cores + core
    offsets = [(a, b) for a in range(1, recs) for b in range(cores)]
    offsets += [(0, b) for b in range(1, cores)]
    has_before, has_after = shot > 0, shot < shots - 1

    def peer(a, b):
        return lax.rem(rec + a, recs), lax.rem(core + b, cores)

    def origin(a, b):
        return lax.rem(rec + recs - a, recs), lax.rem(core + cores - b, cores)

    def rows_of(index, size):
        return pl.ds(pl.multiple_of(index * size, size), size)

    loads = [
        pltpu.make_async_copy(source, target, table_sem.at[k])
        for k, (source, target) in enumerate(
            [
                (model_hbm, model), (trace_t_hbm, trace_table_t), (time_hbm, time_table),
                (record_hbm, record), (time_t_hbm, time_table_t), (trace_hbm, trace_table),
            ]
        )
    ]
    for load in loads:
        load.start()

    barrier = pltpu.get_barrier_semaphore()
    for a, b in offsets:
        to_rec, to_core = peer(a, b)
        pl.semaphore_signal(barrier, inc=1, device_id={"rec": to_rec, "tr": to_core})

    @pl.when(has_before)
    def _():
        pl.semaphore_signal(barrier, inc=1, device_id={"shot": shot - 1})

    @pl.when(has_after)
    def _():
        pl.semaphore_signal(barrier, inc=1, device_id={"shot": shot + 1})

    loads[0].wait()
    loads[1].wait()
    narrow_model[...] = model[...].astype(BF)

    @pl.when(jnp.logical_not(has_before))
    def _():
        tail_in[...] = jnp.zeros_like(tail_in)

    @pl.when(jnp.logical_not(has_after))
    def _():
        head_in[...] = jnp.zeros_like(head_in)

    beside = has_before.astype(jnp.int32) + has_after.astype(jnp.int32)
    pl.semaphore_wait(barrier, len(offsets) + beside)

    delay = dither[0]
    back = jnp.where(delay == 0, 0, span - delay)

    half = traces // PARTS
    near = [j for j, (a, _) in enumerate(offsets) if a == 0]
    far = [j for j, (a, _) in enumerate(offsets) if a > 0]

    def parts_of(j):
        return range(1 if j in near else PARTS)

    def part_rows(j, h):
        return (0, traces) if j in near else (h * half, half)

    def spread_copy(it, j, slot, h):
        to_rec, to_core = peer(*offsets[j])
        rows = pl.ds(*part_rows(j, h))
        return pltpu.make_async_remote_copy(
            spread_out.at[it, j, rows], spread_in.at[it, rows, rows_of(slot, freqs)],
            spread_send.at[it, j, h], spread_recv.at[it, j, h],
            device_id={"rec": to_rec, "tr": to_core},
        )

    def spectra_copy(it, j, slot, h):
        to_rec, to_core = peer(*offsets[j])
        first, count = part_rows(j, h)
        place = pl.ds(pl.multiple_of(slot * traces + first, count), count)
        return pltpu.make_async_remote_copy(
            spectra_out.at[it, j, pl.ds(first, count)], spectra_in.at[it, place],
            spectra_send.at[it, j, h], spectra_recv.at[it, j, h],
            device_id={"rec": to_rec, "tr": to_core},
        )

    def up_copy(it, c):
        rows = pl.ds(c * half, half)
        return pltpu.make_async_remote_copy(
            up_out.at[it, rows], up_in.at[it, rows], part_send.at[it, 0, c],
            part_recv.at[it, 0, c], device_id={"shot": shot + 1},
        )

    def down_copy(it, c):
        rows = pl.ds(c * half, half)
        return pltpu.make_async_remote_copy(
            down_out.at[it, rows], down_in.at[it, rows], part_send.at[it, 1, c],
            part_recv.at[it, 1, c], device_id={"shot": shot - 1},
        )

    def tail_copy(it, c):
        rows = pl.ds(c * half, half)
        return pltpu.make_async_remote_copy(
            narrow.at[it, rows, pl.ds(window - jitter, jitter)], tail_in.at[it, rows],
            res_send.at[it, 0, c], res_recv.at[it, 0, c], device_id={"shot": shot + 1},
        )

    def head_copy(it, c):
        rows = pl.ds(c * half, half)
        return pltpu.make_async_remote_copy(
            narrow.at[it, rows], head_in.at[it, rows],
            res_send.at[it, 1, c], res_recv.at[it, 1, c], device_id={"shot": shot - 1},
        )

    for it in range(ITERS):
        for j, (a, b) in enumerate(offsets):
            to_rec, to_core = peer(a, b)
            block = dot(trace_table_t[rows_of(to_rec * cores + to_core, traces), :], narrow_model[...])
            spread_out[it, j] = block.astype(BF)
            spread_copy(it, j, me, 0).start()
        for h in range(1, PARTS):
            for j in far:
                spread_copy(it, j, me, h).start()
        own = dot(trace_table_t[rows_of(me, traces), :], narrow_model[...]).astype(BF)
        spread_in[it, :, rows_of(me, freqs)] = own
        if it == 0:
            loads[2].wait()
            loads[3].wait()

        def add_blocks(from_rec, rows, first):
            depth = rows_of(from_rec, cores * freqs)

            @pl.loop(0, time_len // TILE)
            def _(i):
                columns = pl.ds(pl.multiple_of(i * TILE, TILE), TILE)
                term = dot(spread_in[it, rows, depth], time_table[depth, columns])
                if first:
                    shot_sum[rows, columns] = term
                else:
                    shot_sum[rows, columns] += term

        def await_blocks(js, h):
            for j in js:
                from_rec, from_core = origin(*offsets[j])
                spread_copy(it, j, from_rec * cores + from_core, h).wait_recv()

        await_blocks(near, 0)
        add_blocks(rec, pl.ds(0, traces), True)
        for h in range(PARTS):
            for a in range(1, recs):
                await_blocks([j for j in far if offsets[j][0] == a], h)
                add_blocks(lax.rem(rec + recs - a, recs), pl.ds(h * half, half), False)

            for c in range(h, h + 1):
                rows = pl.ds(c * half, half)
                data = jnp.concatenate([shot_sum[rows, :], jnp.zeros((half, jitter), F32)], axis=1)
                data = pltpu.roll(data, delay, 1)
                up_out[it, rows, :] = data[:, high:].astype(BF)
                down_out[it, rows, :] = data[:, :jitter].astype(BF)
                residual[rows, :] = record[rows, :] - data[:, jitter:high]

                @pl.when(has_after)
                def _():
                    up_copy(it, c).start()

                @pl.when(has_before)
                def _():
                    down_copy(it, c).start()

        for c in range(PARTS):
            rows = pl.ds(c * half, half)

            @pl.when(has_before)
            def _():
                up_copy(it, c).wait_recv()
                residual[rows, :] -= up_in[it, rows, :].astype(F32)

            @pl.when(has_after)
            def _():
                down_copy(it, c).wait_recv()
                residual[rows, pl.ds(window - jitter, jitter)] -= down_in[it, rows, :].astype(F32)

            narrow[it, rows, :] = residual[rows, :].astype(BF)

            @pl.when(has_before)
            def _():
                head_copy(it, c).start()

            @pl.when(has_after)
            def _():
                tail_copy(it, c).start()

        if it == 0:
            loads[4].wait()
            loads[5].wait()
        for h in range(PARTS):
            for c in range(h, h + 1):
                rows = pl.ds(c * half, half)

                @pl.when(has_before)
                def _():
                    tail_copy(it, c).wait_recv()

                @pl.when(has_after)
                def _():
                    head_copy(it, c).wait_recv()

                data = jnp.concatenate(
                    [tail_in[it, rows, :], narrow[it, rows, :], head_in[it, rows, :]], axis=1
                ).astype(F32)
                windows[rows, :] = pltpu.roll(data, back, 1)[:, :time_len].astype(BF)

            rows = pl.ds(h * half, half)
            for j in far:
                to_rec, to_core = peer(*offsets[j])
                columns = rows_of(to_rec * cores + to_core, freqs)
                spectra_out[it, j, rows] = dot(windows[rows, :], time_table_t[:, columns]).astype(BF)
                spectra_copy(it, j, me, h).start()

        for j in near:
            to_rec, to_core = peer(*offsets[j])
            columns = rows_of(to_rec * cores + to_core, freqs)
            spectra_out[it, j] = dot(windows[...], time_table_t[:, columns]).astype(BF)
            spectra_copy(it, j, me, 0).start()
        own = dot(windows[...], time_table_t[:, rows_of(me, freqs)]).astype(BF)
        spectra_in[it, rows_of(me, traces)] = own

        for a in range(recs):
            for j, (away, _) in enumerate(offsets):
                if away == a:
                    from_rec, from_core = origin(*offsets[j])
                    for h in parts_of(j):
                        spectra_copy(it, j, from_rec * cores + from_core, h).wait_recv()
            part = rows_of(lax.rem(rec + recs - a, recs), cores * traces)
            last = a == recs - 1

            @pl.loop(0, model.shape[0] // 128)
            def _(i):
                out_rows = pl.ds(pl.multiple_of(i * 128, 128), 128)
                grad = dot(trace_table[out_rows, part], spectra_in[it, part])
                value = model[out_rows, :] + 0.5 * grad
                if last:
                    value = value - jnp.clip(value, -0.3, 0.3)
                    narrow_model[out_rows, :] = value.astype(BF)
                model[out_rows, :] = value

    for it in range(ITERS):
        for j in range(len(offsets)):
            for h in parts_of(j):
                spread_copy(it, j, me, h).wait_send()
                spectra_copy(it, j, me, h).wait_send()
        for c in range(PARTS):

            @pl.when(has_after)
            def _():
                up_copy(it, c).wait_send()
                tail_copy(it, c).wait_send()

            @pl.when(has_before)
            def _():
                down_copy(it, c).wait_send()
                head_copy(it, c).wait_send()


def shards(model_init, record, activation_dither):
    _, waves, freqs = model_init.shape
    traces, window = record.shape
    recs, cores, shots = lax.axis_size("rec"), lax.axis_size("tr"), lax.axis_size("shot")
    group = recs * cores
    time_len = freqs * group
    jitter = time_len // 4
    time_table, trace_table = cosine_table(time_len), cosine_table(waves)
    vmem, hbm = pl.BlockSpec(memory_space=pltpu.VMEM), pl.BlockSpec(memory_space=pl.ANY)
    dma = pltpu.SemaphoreType.DMA
    model, residual = pl.pallas_call(
        functools.partial(kernel, (recs, cores, shots, time_len, freqs, traces, window)),
        out_shape=[
            jax.ShapeDtypeStruct((waves, freqs), F32),
            jax.ShapeDtypeStruct((traces, window), F32),
        ],
        in_specs=[pl.BlockSpec(memory_space=pltpu.SMEM)] + [hbm] * 6,
        out_specs=[vmem, vmem],
        scratch_shapes=[
            pltpu.VMEM((traces, window), F32),
            pltpu.VMEM((waves, waves), BF),
            pltpu.VMEM((waves, waves), BF),
            pltpu.VMEM((time_len, time_len), BF),
            pltpu.VMEM((time_len, time_len), BF),
            pltpu.VMEM((waves, freqs), BF),
            pltpu.VMEM((ITERS, group - 1, traces, freqs), BF),
            pltpu.VMEM((ITERS, traces, group * freqs), BF),
            pltpu.VMEM((traces, time_len), F32),
            pltpu.VMEM((ITERS, traces, time_len - window), BF),
            pltpu.VMEM((ITERS, traces, jitter), BF),
            pltpu.VMEM((ITERS, traces, time_len - window), BF),
            pltpu.VMEM((ITERS, traces, jitter), BF),
            pltpu.VMEM((ITERS, traces, window), BF),
            pltpu.VMEM((ITERS, traces, jitter), BF),
            pltpu.VMEM((ITERS, traces, window), BF),
            pltpu.VMEM((traces, time_len), BF),
            pltpu.VMEM((ITERS, group - 1, traces, freqs), BF),
            pltpu.VMEM((ITERS, group * traces, freqs), BF),
            dma((6,)),
            dma((ITERS, group - 1, PARTS)),
            dma((ITERS, group - 1, PARTS)),
            dma((ITERS, 2, PARTS)),
            dma((ITERS, 2, PARTS)),
            dma((ITERS, 2, PARTS)),
            dma((ITERS, 2, PARTS)),
            dma((ITERS, group - 1, PARTS)),
            dma((ITERS, group - 1, PARTS)),
        ],
        compiler_params=pltpu.CompilerParams(
            collective_id=0, has_side_effects=True, vmem_limit_bytes=48 * 1024 * 1024
        ),
        name="deblend",
    )(
        activation_dither, model_init[0], record, jnp.asarray(trace_table),
        jnp.asarray(np.ascontiguousarray(trace_table.T)), jnp.asarray(time_table),
        jnp.asarray(np.ascontiguousarray(time_table.T)),
    )
    return model[None], residual


def solution(mesh):
    return jax.shard_map(
        shards,
        mesh=mesh,
        in_specs=(
            P(("swath", "shot"), None, ("rec", "tr")),
            P(("rec", "tr"), ("swath", "shot")),
            P(("swath", "shot")),
        ),
        out_specs=(P(("swath", "shot"), None, ("rec", "tr")), P(("rec", "tr"), ("swath", "shot"))),
        check_vma=False,
    )
```

time: 65.7 us -> 59.7 us (0.909)
  Pallas kernels: 58 us -> 52 us
    pallas_call x1, Pallas kernels: 58 us -> 52 us  [shards(): pl.pallas_call(functools.partial(kernel, (recs, cores, shots, time_len, f...]
where the time goes in v3:
time: 59.7 us; the launch traced here: 59.4 us
  Pallas kernels  52 us (87%)
  local copies, waits for them, and re-layouts  6.11 us (10%)
  between operations  1.3 us (2%)
    pallas_call x1, Pallas kernels, shards(): pl.pallas_call(functools.partial(kernel, (recs, cores, shots, time_len, f...  52 us
    unnamed x10, local copies, waits for them, and re-layouts  6.11 us

profile of v3, /device:TPU:1, one launch (start us, length us, event | category | flops | bytes accessed | tf_op | source)
XLA Modules:
  0.0 59.4 jit_solution(10510510012584371342)
XLA Ops:
  1.3 0.0 copy-start
  1.3 1.2 %copy-done = f32[1,512,512]{2,1,0:T(8,128)S(1)} copy-done((f32[1,512,512]{2,1,0:T(8,128)S(1)}, f32[1,512,512]{2,1,0:T(8,128)}, u32[]{:S(2)}) %copy-start) | copy-done | bytes 1048600
  2.5 0.0 copy-start.1
  2.5 1.0 %copy-done.1 = f32[128,1024]{1,0:T(8,128)S(1)} copy-done((f32[128,1024]{1,0:T(8,128)S(1)}, f32[128,1024]{1,0:T(8,128)}, u32[]{:S(2)}) %copy-start.1) | copy-done | bytes 524312
  3.5 0.0 copy-start.2
  3.5 1.0 %copy-done.2 = bf16[512,512]{1,0:T(8,128)(2,1)S(1)} copy-done((bf16[512,512]{1,0:T(8,128)(2,1)S(1)}, bf16[512,512]{1,0:T(8,128)(2,1)}, u32[]{:S(2)}) %copy-start.2) | copy-done | bytes 524312
  4.6 0.0 copy-start.3
  4.6 1.0 %copy-done.3 = bf16[512,512]{1,0:T(8,128)(2,1)S(1)} copy-done((bf16[512,512]{1,0:T(8,128)(2,1)S(1)}, bf16[512,512]{1,0:T(8,128)(2,1)}, u32[]{:S(2)}) %copy-start.3) | copy-done | bytes 524312
  5.6 52.0 %deblend.1 = (f32[512,512]{1,0:T(8,128)S(1)}, f32[128,1024]{1,0:T(8,128)S(1)}) custom-call(s32[1]{0:T(128)S(6)} %copy.11.dither, f32[512,512]{1,0:T(8,128)S(1)} %bitcast.2, f32[128,1024]{1,0:T(8,128)S(1)} %copy-done.1, bf16[512,512]{1,0:T(8,128)(2,1)S(1)} %copy-done.3, bf16[512,512]{1,0:T(8,128)(2,1)S(1)} %copy-done.2, ...), custom_call_target="tpu_custom_call" | custom-call | tf_op jit(solution)/shard_map/deblend/pallas_call | solution.py:320
  57.6 1.0 %copy.12 = f32[1,512,512]{2,1,0:T(8,128)} copy(f32[1,512,512]{2,1,0:T(8,128)S(1)} %bitcast.3) | data formatting | bytes 2097152
  58.6 0.8 %copy.13 = f32[128,1024]{1,0:T(8,128)} copy(f32[128,1024]{1,0:T(8,128)S(1)} %get-tuple-element.9) | data formatting | bytes 1048576
Async XLA Ops:
  1.3 1.2 %copy-start = (f32[1,512,512]{2,1,0:T(8,128)S(1)}, f32[1,512,512]{2,1,0:T(8,128)}, u32[]{:S(2)}) copy-start(f32[1,512,512]{2,1,0:T(8,128)} %param.7) | copy-start | bytes 3145732
  2.5 1.0 %copy-start.1 = (f32[128,1024]{1,0:T(8,128)S(1)}, f32[128,1024]{1,0:T(8,128)}, u32[]{:S(2)}) copy-start(f32[128,1024]{1,0:T(8,128)} %record_hbm.1) | copy-start | bytes 1572868
  3.5 1.0 %copy-start.2 = (bf16[512,512]{1,0:T(8,128)(2,1)S(1)}, bf16[512,512]{1,0:T(8,128)(2,1)}, u32[]{:S(2)}) copy-start(bf16[512,512]{1,0:T(8,128)(2,1)} %constant.9.clone.trace_t_hbm) | copy-start | bytes 1572868
  4.6 1.0 %copy-start.3 = (bf16[512,512]{1,0:T(8,128)(2,1)S(1)}, bf16[512,512]{1,0:T(8,128)(2,1)}, u32[]{:S(2)}) copy-start(bf16[512,512]{1,0:T(8,128)(2,1)} %constant.8.clone.trace_hbm) | copy-start | bytes 1572868

commit v4 on v3

--- a/solution.py
+++ b/solution.py
@@ -11,7 +11,7 @@
 from jax.sharding import PartitionSpec as P
 
 ITERS = 2
-PARTS = 2
+PARTS = 4
 TILE = 1024
 BF = jnp.bfloat16
 F32 = jnp.float32
@@ -172,9 +172,7 @@
             loads[2].wait()
             loads[3].wait()
 
-        def add_blocks(from_rec, rows, first):
-            depth = rows_of(from_rec, cores * freqs)
-
+        def add_blocks(depth, rows, first):
             @pl.loop(0, time_len // TILE)
             def _(i):
                 columns = pl.ds(pl.multiple_of(i * TILE, TILE), TILE)
@@ -190,11 +188,13 @@
                 spread_copy(it, j, from_rec * cores + from_core, h).wait_recv()
 
         await_blocks(near, 0)
-        add_blocks(rec, pl.ds(0, traces), True)
+        add_blocks(rows_of(rec, cores * freqs), pl.ds(0, traces), True)
         for h in range(PARTS):
-            for a in range(1, recs):
-                await_blocks([j for j in far if offsets[j][0] == a], h)
-                add_blocks(lax.rem(rec + recs - a, recs), pl.ds(h * half, half), False)
+            for j in far:
+                await_blocks([j], h)
+                from_rec, from_core = origin(*offsets[j])
+                slot = from_rec * cores + from_core
+                add_blocks(rows_of(slot, freqs), pl.ds(h * half, half), False)
 
             for c in range(h, h + 1):
                 rows = pl.ds(c * half, half)

time: 59.7 us -> 57.7 us (0.966)
  Pallas kernels: 52 us -> 49.8 us
    pallas_call x1, Pallas kernels: 52 us -> 49.8 us  [shards(): pl.pallas_call(functools.partial(kernel, (recs, cores, shots, time_len, f...]
where the time goes in v4:
time: 57.7 us; the launch traced here: 57.2 us
  Pallas kernels  49.8 us (86%)
  local copies, waits for them, and re-layouts  6.11 us (11%)
  between operations  1.3 us (2%)
    pallas_call x1, Pallas kernels, shards(): pl.pallas_call(functools.partial(kernel, (recs, cores, shots, time_len, f...  49.8 us
    unnamed x10, local copies, waits for them, and re-layouts  6.11 us

profile of v4, /device:TPU:1, one launch (start us, length us, event | category | flops | bytes accessed | tf_op | source)
XLA Modules:
  0.0 57.2 jit_solution(14442105524741650941)
XLA Ops:
  1.3 0.0 copy-start
  1.3 1.2 %copy-done = f32[1,512,512]{2,1,0:T(8,128)S(1)} copy-done((f32[1,512,512]{2,1,0:T(8,128)S(1)}, f32[1,512,512]{2,1,0:T(8,128)}, u32[]{:S(2)}) %copy-start) | copy-done | bytes 1048600
  2.5 0.0 copy-start.1
  2.5 1.0 %copy-done.1 = f32[128,1024]{1,0:T(8,128)S(1)} copy-done((f32[128,1024]{1,0:T(8,128)S(1)}, f32[128,1024]{1,0:T(8,128)}, u32[]{:S(2)}) %copy-start.1) | copy-done | bytes 524312
  3.5 0.0 copy-start.2
  3.5 1.0 %copy-done.2 = bf16[512,512]{1,0:T(8,128)(2,1)S(1)} copy-done((bf16[512,512]{1,0:T(8,128)(2,1)S(1)}, bf16[512,512]{1,0:T(8,128)(2,1)}, u32[]{:S(2)}) %copy-start.2) | copy-done | bytes 524312
  4.6 0.0 copy-start.3
  4.6 1.0 %copy-done.3 = bf16[512,512]{1,0:T(8,128)(2,1)S(1)} copy-done((bf16[512,512]{1,0:T(8,128)(2,1)S(1)}, bf16[512,512]{1,0:T(8,128)(2,1)}, u32[]{:S(2)}) %copy-start.3) | copy-done | bytes 524312
  5.6 49.8 %deblend.1 = (f32[512,512]{1,0:T(8,128)S(1)}, f32[128,1024]{1,0:T(8,128)S(1)}) custom-call(s32[1]{0:T(128)S(6)} %copy.11.dither, f32[512,512]{1,0:T(8,128)S(1)} %bitcast.2, f32[128,1024]{1,0:T(8,128)S(1)} %copy-done.1, bf16[512,512]{1,0:T(8,128)(2,1)S(1)} %copy-done.3, bf16[512,512]{1,0:T(8,128)(2,1)S(1)} %copy-done.2, ...), custom_call_target="tpu_custom_call" | custom-call | tf_op jit(solution)/shard_map/deblend/pallas_call | solution.py:320
  55.4 1.0 %copy.12 = f32[1,512,512]{2,1,0:T(8,128)} copy(f32[1,512,512]{2,1,0:T(8,128)S(1)} %bitcast.3) | data formatting | bytes 2097152
  56.4 0.8 %copy.13 = f32[128,1024]{1,0:T(8,128)} copy(f32[128,1024]{1,0:T(8,128)S(1)} %get-tuple-element.9) | data formatting | bytes 1048576
Async XLA Ops:
  1.3 1.2 %copy-start = (f32[1,512,512]{2,1,0:T(8,128)S(1)}, f32[1,512,512]{2,1,0:T(8,128)}, u32[]{:S(2)}) copy-start(f32[1,512,512]{2,1,0:T(8,128)} %param.7) | copy-start | bytes 3145732
  2.5 1.0 %copy-start.1 = (f32[128,1024]{1,0:T(8,128)S(1)}, f32[128,1024]{1,0:T(8,128)}, u32[]{:S(2)}) copy-start(f32[128,1024]{1,0:T(8,128)} %record_hbm.1) | copy-start | bytes 1572868
  3.5 1.0 %copy-start.2 = (bf16[512,512]{1,0:T(8,128)(2,1)S(1)}, bf16[512,512]{1,0:T(8,128)(2,1)}, u32[]{:S(2)}) copy-start(bf16[512,512]{1,0:T(8,128)(2,1)} %constant.9.clone.trace_t_hbm) | copy-start | bytes 1572868
  4.6 1.0 %copy-start.3 = (bf16[512,512]{1,0:T(8,128)(2,1)S(1)}, bf16[512,512]{1,0:T(8,128)(2,1)}, u32[]{:S(2)}) copy-start(bf16[512,512]{1,0:T(8,128)(2,1)} %constant.8.clone.trace_hbm) | copy-start | bytes 1572868
